TPU v7x, 512 devices: a whole 4x4x16 slice. The times are simulated.
512 devices in a mesh: dp: 64 (over z, x), sub: 8 (over y, core).
Axes of the slice: x: 4, y: 4, z: 16, core: 2. Of those that a mesh axis runs over, the one named last changes fastest.
Arguments:
- points: bfloat16 [262144, 256], P(('dp', 'sub'))
- candidates: int32 [4, 768], replicated, may hold values from 0 to 262143, as said below
- owner_slot: int32 [3072], replicated, may hold values from 0 to 3071, each once
Outputs:
- centroids: float32 [3072, 256], P(('dp', 'sub'))
- masses: float32 [3072], P(('dp', 'sub'))
- min_dist: float32 [262144], P(('dp', 'sub'))
Inputs may be any that keep to these rules, and one draw needn't show every extreme that they name: In each round the candidates are distinct rows; no device's block of 512 rows holds more than 8 candidates of one round, and in each round some device's block holds exactly 8.
All inputs are finite; a program needn't handle non-finite values.
Results may differ from a plain program's by a relative error of at most 0.00055.
Values may be sent and summed in bfloat16 or wider, within the bound.
A program may use at most 64 MiB of HBM per device.

v0:
```python
import jax
import jax.numpy as jnp
from jax import lax
from jax.sharding import PartitionSpec as P


def pick_rows(round_rows, points, my_device):
    row_count = points.shape[0]
    flat_rows = round_rows.reshape(-1)
    owner_dev = flat_rows // row_count
    local_row = flat_rows % row_count
    mine = owner_dev == my_device
    picked = jnp.where(
        mine[:, None], points[local_row].astype(jnp.float32), jnp.zeros((), jnp.float32)
    )
    return lax.psum(picked, ("dp", "sub")).astype(jnp.bfloat16)


def on_device(points, candidates, owner_slot):
    row_count = points.shape[0]
    width_dim = points.shape[1]
    round_count = candidates.shape[0]
    my_device = lax.axis_index(("dp", "sub"))
    block_rows = min(512, row_count)
    point_norm = jnp.sum(points.astype(jnp.float32) ** 2, axis=1)
    chosen_list = [
        pick_rows(candidates[which_round : which_round + 1], points, my_device)
        for which_round in range(round_count)
    ]
    nearest_parts = [jnp.full((block_rows,), 3e38, jnp.float32)]
    sums_parts = []
    mass_parts = []
    for which_round in range(round_count):
        chosen = chosen_list[which_round]
        cand_norm = jnp.sum(chosen.astype(jnp.float32) ** 2, axis=1)
        dots = lax.dot_general(
            points, chosen, (((1,), (1,)), ((), ())), preferred_element_type=jnp.float32
        )
        dist = point_norm[:, None] + cand_norm[None, :] - 2.0 * dots
        nearest_parts[0] = jnp.minimum(nearest_parts[0], jnp.min(dist, axis=1))
        kernel = jnp.exp(-dist / 0.25).astype(jnp.bfloat16)
        sums_round = lax.dot_general(
            kernel, points, (((0,), (0,)), ((), ())), preferred_element_type=jnp.float32
        )
        mass_round = jnp.sum(kernel.astype(jnp.float32), axis=0)
        sums_parts.append(sums_round)
        mass_parts.append(mass_round)
    partial_sums = jnp.concatenate(sums_parts, axis=0)
    partial_mass = jnp.concatenate(mass_parts, axis=0)
    total_rows = partial_sums.shape[0]
    placed_sums = jnp.zeros((total_rows, width_dim), jnp.float32).at[owner_slot].set(partial_sums)
    placed_mass = jnp.zeros((total_rows,), jnp.float32).at[owner_slot].set(partial_mass)
    summed, masses = (
        lax.psum_scatter(placed_sums, ("dp", "sub"), scatter_dimension=0, tiled=True),
        lax.psum_scatter(placed_mass, ("dp", "sub"), scatter_dimension=0, tiled=True),
    )
    centroids = summed / masses[:, None]
    min_dist = nearest_parts[0]
    return (centroids, masses, min_dist)


def solution(mesh):
    placed = (P(("dp", "sub"), None), P(), P())
    return jax.shard_map(
        on_device,
        mesh=mesh,
        in_specs=placed,
        out_specs=(P(("dp", "sub"), None), P(("dp", "sub")), P(("dp", "sub"))),
        check_vma=False,
    )
```

profile of v0, /device:TPU:2, one launch (start us, length us, event | category | flops | bytes accessed | tf_op | source)
XLA Modules:
  0.0 728.4 jit_solution(3182562303138796579)
XLA Ops:
  7.2 0.9 slice_reduce_fusion.3
  8.1 0.9 fusion.31
  9.1 1.1 multiply_reduce_fusion.4
  10.2 0.7 compare_select_fusion
  10.9 2.7 gather_fusion.3
  13.6 2.7 gather_fusion.1
  16.5 0.2 convert_select_fusion
  16.6 2.7 gather_fusion.2
  19.5 3.3 gather_fusion
  22.8 1.2 convert_select_fusion.3
  23.9 188.3 %all-reduce.7 = (bf16[768,256]{1,0:T(8,128)(2,1)}, bf16[768,256]{1,0:T(8,128)(2,1)}, bf16[768,256]{1,0:T(8,128)(2,1)}, bf16[768,256]{1,0:T(8,128)(2,1)}) all-reduce(f32[768,256]{1,0:T(8,128)S(1)} %convert_select_fusion, f32[768,256]{1,0:T(8,128)S(1)} %convert_select_fusion.1, ...), channel_id=1, replica_groups=mesh['dp'=64,'sub'=8] {'dp','sub'}, use_global_device_ids=true, to_apply=%region_7.8 | all-reduce | flops 786432 | bytes 4718592 | tf_op jit(solution)/shard_map/psum | solution.py:16
  212.2 1.2 multiply_reduce_fusion
  213.4 1.2 multiply_reduce_fusion.1
  214.6 1.2 multiply_reduce_fusion.2
  215.8 1.2 multiply_reduce_fusion.3
  217.0 0.7 fusion.43
  217.7 0.4 fusion.13
  218.1 0.6 copy-done.3
  218.7 0.7 fusion.44
  219.4 0.4 fusion.14
  219.7 0.6 copy-done.2
  220.4 0.7 fusion.45
  221.0 0.4 fusion.15
  221.4 0.6 copy-done.1
  222.0 0.7 fusion.46
  222.7 0.4 fusion.16
  223.1 17.2 %scatter_custom_fusion = f32[3072,256]{1,0:T(8,128)} fusion(s32[3072]{0:T(1024)S(1)} %compare_select_fusion, f32[768,256]{1,0:T(8,128)S(1)} %fusion.16, f32[]{:T(128)} %constant.110, f32[768,256]{1,0:T(8,128)S(1)} %fusion.15, f32[768,256]{1,0:T(8,128)S(1)} %fusion.14, f32[768,256]{1,0:T(8,128)S(1)} %fusion.13, f32[]{:T(128)} %constant.80.clone.1), kind=kCustom, calls=%fused_computation.6 | custom fusion | flops 2359296 | bytes 6291464 | tf_op jit(solution)/shard_map/scatter | solution.py:51
  240.3 11.8 %scatter_custom_fusion.1 = f32[3072]{0:T(1024)S(1)} fusion(s32[3072]{0:T(1024)S(1)} %compare_select_fusion, f32[3072]{0:T(1024)S(1)} %pad_maximum_fusion, f32[]{:T(128)} %constant.80.clone.1), kind=kCustom, calls=%fused_computation.63 | custom fusion | bytes 12292 | tf_op jit(solution)/shard_map/scatter | solution.py:52
  252.1 100.5 %all-reduce.1 = f32[3072]{0:T(1024)S(1)} all-reduce(f32[3072]{0:T(1024)S(1)} %scatter_custom_fusion.1), channel_id=3, replica_groups=mesh['dp'=64,'sub'=8] {'dp','sub'}, use_global_device_ids=true, to_apply=%region_16.17.clone | all-reduce | flops 3072 | bytes 24576
  352.8 0.6 minimum_minimum_fusion
  353.3 366.8 %all-reduce.6.cloned.1.call-done = f32[3072,256]{1,0:T(8,128)} async-done(((f32[3072,256]{1,0:T(8,128)}), f32[3072,256]{1,0:T(8,128)}) %all-reduce.6.cloned.1.call-update) | async-done | bytes 3145744
  720.1 1.4 dynamic-slice_divide_fusion
  (19 shorter events, 0.5 us)
Async XLA Ops:
  7.2 3.7 copy-start
  7.2 712.9 %all-reduce.6.cloned.1.call-start = ((), (), s32[]{:S(2)}) async-start(), calls=%async_computation | async-start | bytes 6291456
  212.2 4.8 copy-start.4
  217.7 1.0 copy-start.3
  219.4 1.0 copy-start.2
  221.0 1.0 copy-start.1
  352.8 368.8 %copy-start.5 = (f32[6]{0:T(128)}, f32[6]{0:T(128)S(1)}, u32[]{:S(2)}) copy-start(f32[6]{0:T(128)S(1)} %dynamic-slice.1) | copy-start | bytes 76
Sparse Core Ops, SparseCore 0:
  240.4 479.6 all-reduce.5
where the time goes:
time: 729 us; the launch traced here: 728 us
  waiting for transfers between devices  367 us (50%)
  blocking collectives  289 us (40%)
  other arithmetic  28.4 us (4%)
  local copies, waits for them, and re-layouts  25.9 us (4%)
  between operations  14.3 us (2%)
    unnamed x2, waiting for transfers between devices  367 us
    psum x1, blocking collectives, pick_rows(): return lax.psum(picked, ('dp', 'sub')).astype(jnp.bfloat16)  188 us
    unnamed x1, blocking collectives  101 us
    scatter x1, other arithmetic, on_device(): jnp.zeros((total_rows, width_dim), jnp.float32).at[owner_slot]  17.2 us
  transfers between devices with their start and end apart: 1, of which 1 were waited for; matrix products, arithmetic and copies ran while one was open for 2% of the time, Pallas kernels for 0%

commit v1 on v0

--- a/solution.py
+++ b/solution.py
@@ -2,6 +2,10 @@
 import jax.numpy as jnp
 from jax import lax
 from jax.sharding import PartitionSpec as P
+
+
+def samples_manage(message, mesh_dim, link_axis):
+    return lax.psum(lax.psum(message, mesh_dim), link_axis)
 
 
 def pick_rows(round_rows, points, my_device):
@@ -13,7 +17,7 @@
     picked = jnp.where(
         mine[:, None], points[local_row].astype(jnp.float32), jnp.zeros((), jnp.float32)
     )
-    return lax.psum(picked, ("dp", "sub")).astype(jnp.bfloat16)
+    return samples_manage(picked, "sub", "dp").astype(jnp.bfloat16)
 
 
 def on_device(points, candidates, owner_slot):

time: 729 us -> 940 us (1.29)
  blocking collectives: 289 us -> 414 us
  waiting for transfers between devices: 367 us -> 457 us
    psum x1, blocking collectives: 188 us -> 311 us  [samples_manage(): return lax.psum(lax.psum(message, mesh_dim), link_axis)]
    psum x0 -> x1, waiting for transfers between devices: none -> 88.7 us  [samples_manage(): return lax.psum(lax.psum(message, mesh_dim), link_axis)]
    unnamed x2 -> x3, waiting for transfers between devices: 367 us -> 368 us
  transfers between devices with their start and end apart: 1 -> 2, of which waited for: 1 -> 2; matrix products, arithmetic and copies ran while one was open for 2% -> 1% of each run, Pallas kernels for 0% -> 0%
where the time goes in v1:
time: 940 us; the launch traced here: 939 us
  waiting for transfers between devices  457 us (49%)
  blocking collectives  414 us (44%)
  other arithmetic  25.3 us (3%)
  local copies, waits for them, and re-layouts  24.4 us (3%)
  between operations  14.2 us (2%)
    unnamed x3, waiting for transfers between devices  368 us
    psum x1, blocking collectives, samples_manage(): return lax.psum(lax.psum(message, mesh_dim), link_axis)  311 us
    unnamed x1, blocking collectives  103 us
    psum x1, waiting for transfers between devices, samples_manage(): return lax.psum(lax.psum(message, mesh_dim), link_axis)  88.7 us
  transfers between devices with their start and end apart: 2, of which 2 were waited for; matrix products, arithmetic and copies ran while one was open for 1% of the time, Pallas kernels for 0%

profile of v1, /device:TPU:2, one launch (start us, length us, event | category | flops | bytes accessed | tf_op | source)
XLA Modules:
  0.0 939.3 jit_solution(9356428414461727601)
XLA Ops:
  7.2 0.9 slice_reduce_fusion.3
  8.1 0.9 fusion.31
  9.1 3.1 gather_fusion.3
  12.3 2.7 gather_fusion.1
  14.9 2.7 gather_fusion.2
  17.6 2.7 gather_fusion
  20.3 1.1 convert_select_fusion.2
  21.4 1.0 convert_select_fusion
  22.4 1.0 convert_select_fusion.1
  23.5 1.1 convert_select_fusion.3
  24.6 0.1 multiply_reduce_fusion.4
  24.8 0.5 copy-done.1
  25.3 88.7 %all-reduce.10.cloned.1.call-done = (f32[768,256]{1,0:T(8,128)}, f32[768,256]{1,0:T(8,128)}, f32[768,256]{1,0:T(8,128)}, f32[768,256]{1,0:T(8,128)}) async-done(((f32[768,256]{1,0:T(8,128)}, f32[768,256]{1,0:T(8,128)}, f32[768,256]{1,0:T(8,128)}, f32[768,256]{1,0:T(8,128)}), (f32[768,256]{1,0:T(8,128)}, f32[768,256]{1,0:T(8,128)}, f32[768,256]{1,0:T(8,128)}, ...) | async-done | bytes 3145744 | tf_op jit(solution)/shard_map/psum | solution.py:8
  113.9 310.9 %all-reduce.11 = (bf16[768,256]{1,0:T(8,128)(2,1)S(1)}, bf16[768,256]{1,0:T(8,128)(2,1)S(1)}, bf16[768,256]{1,0:T(8,128)(2,1)S(1)}, bf16[768,256]{1,0:T(8,128)(2,1)S(1)}) all-reduce(f32[768,256]{1,0:T(8,128)} %get-tuple-element.23, f32[768,256]{1,0:T(8,128)} %get-tuple-element.24, ...), channel_id=1, replica_groups=mesh['dp'=64,'sub'=8] {'dp'}, use_global_device_ids=true, to_apply=%region_11.12 | all-reduce | flops 786432 | bytes 4718592 | tf_op jit(solution)/shard_map/psum | solution.py:8
  424.9 0.2 multiply_reduce_fusion
  425.0 0.2 multiply_reduce_fusion.1
  425.2 0.2 multiply_reduce_fusion.2
  425.4 0.2 multiply_reduce_fusion.3
  425.6 0.7 fusion.43
  426.3 0.4 fusion.13
  426.7 0.7 fusion.44
  427.4 0.4 fusion.14
  427.7 0.7 fusion.45
  428.4 0.4 fusion.15
  428.8 0.7 fusion.46
  429.5 0.4 fusion.16
  429.9 17.2 %scatter_custom_fusion = f32[3072,256]{1,0:T(8,128)} fusion(s32[3072]{0:T(1024)S(1)} %compare_select_fusion, f32[768,256]{1,0:T(8,128)S(1)} %fusion.16, f32[]{:T(128)} %constant.110, f32[768,256]{1,0:T(8,128)S(1)} %fusion.15, f32[768,256]{1,0:T(8,128)S(1)} %fusion.14, f32[768,256]{1,0:T(8,128)S(1)} %fusion.13, f32[]{:T(128)} %constant.80.clone.1), kind=kCustom, calls=%fused_computation.6 | custom fusion | flops 2359296 | bytes 6291464 | tf_op jit(solution)/shard_map/scatter | solution.py:55
  447.1 11.8 %scatter_custom_fusion.1 = f32[3072]{0:T(1024)S(1)} fusion(s32[3072]{0:T(1024)S(1)} %compare_select_fusion, f32[3072]{0:T(1024)S(1)} %pad_maximum_fusion, f32[]{:T(128)} %constant.80.clone.1), kind=kCustom, calls=%fused_computation.63 | custom fusion | bytes 12292 | tf_op jit(solution)/shard_map/scatter | solution.py:56
  458.9 103.5 %all-reduce.1 = f32[3072]{0:T(1024)S(1)} all-reduce(f32[3072]{0:T(1024)S(1)} %scatter_custom_fusion.1), channel_id=3, replica_groups=mesh['dp'=64,'sub'=8] {'dp','sub'}, use_global_device_ids=true, to_apply=%region_20.21.clone | all-reduce | flops 3072 | bytes 24576
  562.5 0.6 minimum_minimum_fusion
  563.1 368.0 %all-reduce.8.cloned.1.call-done = f32[3072,256]{1,0:T(8,128)} async-done(((f32[3072,256]{1,0:T(8,128)}), f32[3072,256]{1,0:T(8,128)}) %all-reduce.8.cloned.1.call-update) | async-done | bytes 3145744
  931.1 1.4 dynamic-slice_divide_fusion
  (16 shorter events, 0.3 us)
Async XLA Ops:
  7.2 106.8 %all-reduce.10.cloned.1.call-start = ((), (), s32[]{:S(2)}) async-start(), calls=%async_computation.1 | async-start | bytes 6291456 | tf_op jit(solution)/shard_map/psum | solution.py:8
  9.1 3.2 copy-start
  24.6 0.7 copy-start.1
  24.6 906.5 %all-reduce.8.cloned.1.call-start = ((), (), s32[]{:S(2)}) async-start(), calls=%async_computation | async-start | bytes 6291456
  562.5 370.0 %copy-start.2 = (f32[6]{0:T(128)}, f32[6]{0:T(128)S(1)}, u32[]{:S(2)}) copy-start(f32[6]{0:T(128)S(1)} %dynamic-slice.1) | copy-start | bytes 76
Sparse Core Ops, SparseCore 0:
  24.7 89.1 all-reduce.9
  447.2 483.8 all-reduce.7
